TPU v7x, 512 devices: a whole 4x8x8 slice. The times are simulated.
512 devices in a mesh: leaf: 8 (over x, core), col: 64 (over z, y).
Axes of the slice: x: 4, y: 8, z: 8, core: 2. Of those that a mesh axis runs over, the one named last changes fastest.
Arguments:
- child_panels: bfloat16 [8, 8192, 2048], P('leaf', 'col'), may hold values from -6 to 6
- child_links: bfloat16 [8, 512, 2048], P('leaf', 'col'), may hold values from -6 to 6
- child_pivots: bfloat16 [8, 1024, 1024], P('leaf', 'col'), may hold values from -6 to 6
- child_inverse: bfloat16 [8, 2, 1024, 1024], P('leaf', None, 'col'), as said below
- block_mask: int32 [8, 64, 2], P('leaf', 'col'), may hold values from 0 to 1, as said below
- row_map: int32 [8, 8192], P('leaf', 'col'), may hold values from 0 to 255, as said below
- parent_panels: bfloat16 [8, 8192, 2048], P('leaf', 'col'), may hold values from -6 to 6
- parent_pivots: bfloat16 [4, 1024, 1024], P(None, 'col'), may hold values from -6 to 6
- parent_inverse: bfloat16 [4, 2, 1024, 1024], P(None, None, 'col'), as said below
Outputs:
- child_factor: bfloat16 [8, 8192, 2048], P('leaf', 'col')
- parent_factor: bfloat16 [8, 8192, 2048], P('leaf', 'col')
Inputs may be any that keep to these rules, and one draw needn't show every extreme that they name: block_mask[f, b, 1] >= block_mask[f, b, 0]: a row block present in a front's first panel is present in its second. `row_map`: within each block of 128 consecutive rows of one front the values are distinct. Each child_inverse[f, k] is lower triangular. Each parent_inverse[p, k] is lower triangular.
All inputs are finite; a program needn't handle non-finite values.
Results may differ from a plain program's by a relative error of at most 0.011.
Values may be sent and summed in bfloat16 or wider, within the bound.
No kernel may reach another device: no remote copies, remote signals or barrier semaphores. Data moves between devices by JAX's collectives and lax.ppermute only.
A program may use at most 64 MiB of HBM per device.

v0:
```python
import jax
import jax.numpy as jnp
from jax import lax
from jax.sharding import PartitionSpec as P


def partner(value, axis, stride):
    return lax.ppermute(value, axis, [(i, i ^ 1 << stride) for i in range(lax.axis_size(axis))])


def times_rows(left_rows, segment):
    return lax.dot_general(
        left_rows, segment, (((1,), (1,)), ((), ())), preferred_element_type=jnp.float32
    )


def masked_products(body_rows, segment):
    return times_rows(body_rows, segment)


def all_products(body_rows, extra_rows, segment):
    main_part = masked_products(body_rows, segment)
    if extra_rows is None:
        return main_part
    return jnp.concatenate([main_part, times_rows(extra_rows, segment)], 0)


def apply_inverse(body_rows, extra_rows, inverse_shard):

    def apply_segment(segment, offset):
        return all_products(body_rows, extra_rows, segment)

    return apply_segment(lax.all_gather(inverse_shard, "col", axis=0, tiled=True), jnp.int32(0))


def apply_factor(body_rows, extra_rows, factor_shard):

    def apply_segment(segment, offset):
        return all_products(body_rows, extra_rows, segment)

    return apply_segment(lax.all_gather(factor_shard, "col", axis=0, tiled=True), jnp.int32(0))


def local(
    child_panels,
    child_links,
    child_pivots,
    child_inverse,
    block_mask,
    row_map,
    parent_panels,
    parent_pivots,
    parent_inverse,
):
    panel_width = child_pivots.shape[2]
    local_rows = child_panels.shape[1]
    row_flags = block_mask[0]
    first_flags = row_flags[:, 0]
    second_flags = row_flags[:, 1]
    keep_first = jnp.repeat(first_flags, 128)[:, None].astype(jnp.bfloat16)
    keep_second = jnp.repeat(second_flags, 128)[:, None].astype(jnp.bfloat16)
    first_input = child_panels[0, :, :panel_width] * keep_first
    second_input = child_panels[0, :, panel_width:] * keep_second
    link_rows = child_links[0]
    pivot_rows = child_pivots[0]
    link_count = link_rows.shape[0]
    extra_first = jnp.concatenate([link_rows[:, :panel_width], pivot_rows], 0)
    first_all = apply_inverse(first_input, extra_first, child_inverse[0, 0]).astype(jnp.bfloat16)
    child_first = first_all[:local_rows]
    link_first = first_all[local_rows : local_rows + link_count]
    pivot_first = first_all[local_rows + link_count :]
    update_terms = apply_factor(child_first, link_first, pivot_first)
    second_source = jnp.concatenate([second_input, link_rows[:, panel_width:]], 0)
    second_rhs = (second_source.astype(jnp.float32) - update_terms).astype(jnp.bfloat16)
    second_all = apply_inverse(
        second_rhs[:local_rows], second_rhs[local_rows:], child_inverse[0, 1]
    ).astype(jnp.bfloat16)
    child_second = second_all[:local_rows]
    link_second = second_all[local_rows:]
    child_factor = jnp.concatenate([child_first, child_second], 1)
    link_factor = jnp.concatenate([link_first, link_second], 1)
    contribution = -apply_factor(child_factor, None, link_factor)
    sibling_bit = lax.axis_index("leaf") % 2
    target_rows = row_map[0]
    placed = (
        jnp.zeros((2 * local_rows, contribution.shape[1]), jnp.float32)
        .at[target_rows]
        .add(contribution)
    )
    own_part = lax.dynamic_slice_in_dim(placed, sibling_bit * local_rows, local_rows, 0)
    sent_part = lax.dynamic_slice_in_dim(placed, (1 - sibling_bit) * local_rows, local_rows, 0)
    received = partner(sent_part, "leaf", 0)
    extension = jnp.where(
        sibling_bit == 0,
        jnp.concatenate([own_part, received], 1),
        jnp.concatenate([received, own_part], 1),
    )
    parent_index = lax.axis_index("leaf") // 2
    parent_pivot_rows = lax.dynamic_index_in_dim(parent_pivots, parent_index, 0, keepdims=False)
    parent_inverses = lax.dynamic_index_in_dim(parent_inverse, parent_index, 0, keepdims=False)
    parent_input = (parent_panels[0, :, :panel_width].astype(jnp.float32) + extension).astype(
        jnp.bfloat16
    )
    parent_all = apply_inverse(parent_input, parent_pivot_rows, parent_inverses[0]).astype(
        jnp.bfloat16
    )
    parent_first = parent_all[:local_rows]
    parent_pivot_first = parent_all[local_rows:]
    parent_update = apply_factor(parent_first, None, parent_pivot_first)
    parent_rhs = (parent_panels[0, :, panel_width:].astype(jnp.float32) - parent_update).astype(
        jnp.bfloat16
    )
    parent_second = apply_inverse(parent_rhs, None, parent_inverses[1]).astype(jnp.bfloat16)
    parent_factor = jnp.concatenate([parent_first, parent_second], 1)
    return (child_factor[None], parent_factor[None])


def solution(mesh):
    return jax.shard_map(
        local,
        mesh=mesh,
        in_specs=(
            P("leaf", "col", None),
            P("leaf", "col", None),
            P("leaf", "col", None),
            P("leaf", None, "col", None),
            P("leaf", "col", None),
            P("leaf", "col"),
            P("leaf", "col", None),
            P(None, "col", None),
            P(None, None, "col", None),
        ),
        out_specs=(P("leaf", "col", None), P("leaf", "col", None)),
        check_vma=False,
    )
```

profile of v0, /device:TPU:2, one launch (start us, length us, event | category | flops | bytes accessed | tf_op | source)
XLA Modules:
  0.0 614.0 jit_solution(18251603384100737075)
XLA Ops:
  7.2 1.5 fusion.71
  8.8 0.7 fusion.72
  9.5 90.5 %all-gather.18.cloned.1.call-done = bf16[1,1,1024,1024]{3,2,1,0:T(8,128)(2,1)} async-done(((bf16[1,1,16,1024]{3,2,1,0:T(8,128)(2,1)}), bf16[1,1,1024,1024]{3,2,1,0:T(8,128)(2,1)}) %all-gather.18.cloned.1.call-update) | async-done | bytes 2097168 | tf_op jit(solution)/shard_map/all_gather | solution.py:33
  100.1 2.4 fusion.27
  102.5 0.6 slice.92
  103.2 0.7 all-gather.20.cloned.1.call-update
  104.0 1.4 constant_dynamic-slice_fusion
  105.5 0.6 fusion.73
  106.1 0.7 multiply_bitcast_fusion
  106.8 1.4 fusion.14
  108.1 75.7 %all-gather.12.cloned.1.call-done = bf16[1024,1024]{1,0:T(8,128)(2,1)} async-done(((bf16[16,1024]{1,0:T(8,128)(2,1)}), bf16[1024,1024]{1,0:T(8,128)(2,1)}) %all-gather.12.cloned.1.call-update) | async-done | bytes 2097168 | tf_op jit(solution)/shard_map/all_gather | solution.py:41
  183.8 2.4 fusion.69
  186.2 0.9 fusion.74
  187.1 80.9 %all-gather.20.cloned.1.call-done = bf16[1,1,1024,1024]{3,2,1,0:T(8,128)(2,1)} async-done(((bf16[1,1,16,1024]{3,2,1,0:T(8,128)(2,1)}), bf16[1,1,1024,1024]{3,2,1,0:T(8,128)(2,1)}) %all-gather.20.cloned.1.call-update) | async-done | bytes 2097168 | tf_op jit(solution)/shard_map/all_gather | solution.py:33
  268.0 2.2 fusion.33
  270.3 0.6 pad_maximum_fusion.2
  271.0 0.5 all-gather.24.cloned.1.call-update
  271.5 79.9 %all-gather.22.cloned.1.call-done = bf16[1,1,1024,1024]{3,2,1,0:T(8,128)(2,1)} async-done(((bf16[1,1,16,1024]{3,2,1,0:T(8,128)(2,1)}), bf16[1,1,1024,1024]{3,2,1,0:T(8,128)(2,1)}) %all-gather.22.cloned.1.call-update) | async-done | bytes 2097168 | tf_op jit(solution)/shard_map/all_gather | solution.py:33
  351.5 2.9 fusion.30
  354.4 0.1 fusion.36
  354.5 0.8 fusion.17
  355.3 80.2 %all-gather.14.cloned.1.call-done = bf16[512,2048]{1,0:T(8,128)(2,1)} async-done(((bf16[8,2048]{1,0:T(8,128)(2,1)}), bf16[512,2048]{1,0:T(8,128)(2,1)}) %all-gather.14.cloned.1.call-update) | async-done | bytes 2097168 | tf_op jit(solution)/shard_map/all_gather | solution.py:41
  435.5 2.4 convolution_negate_fusion
  437.9 1.5 scatter_custom_fusion
  439.4 1.9 collective-permute-start
  441.4 0.8 fusion.40
  442.2 0.7 collective-permute-done
  442.9 2.4 fusion.20
  445.3 73.7 %all-gather.24.cloned.1.call-done = bf16[1,1,1024,1024]{3,2,1,0:T(8,128)(2,1)} async-done(((bf16[1,1,16,1024]{3,2,1,0:T(8,128)(2,1)}), bf16[1,1,1024,1024]{3,2,1,0:T(8,128)(2,1)}) %all-gather.24.cloned.1.call-update) | async-done | bytes 2097168 | tf_op jit(solution)/shard_map/all_gather | solution.py:33
  518.9 83.6 %all-gather.16.cloned.1.call-done = bf16[1024,1024]{1,0:T(8,128)(2,1)} async-done(((bf16[16,1024]{1,0:T(8,128)(2,1)}), bf16[1024,1024]{1,0:T(8,128)(2,1)}) %all-gather.16.cloned.1.call-update) | async-done | bytes 2097168 | tf_op jit(solution)/shard_map/all_gather | solution.py:41
  602.6 3.7 fusion.23
  606.3 0.8 maximum_bitcast_fusion
  (35 shorter events, 0.5 us)
Async XLA Ops:
  7.2 344.3 %copy-start = (bf16[4,16,1024]{2,1,0:T(8,128)(2,1)S(1)}, bf16[4,16,1024]{2,1,0:T(8,128)(2,1)}, u32[]{:S(2)}) copy-start(bf16[4,16,1024]{2,1,0:T(8,128)(2,1)} %param.16) | copy-start | bytes 393220
  7.2 98.3 %copy-start.7 = (s32[1,1,2]{2,1,0:T(1,128)S(1)}, s32[1,1,2]{2,1,0:T(1,128)}, u32[]{:S(2)}) copy-start(s32[1,1,2]{2,1,0:T(1,128)} %param.13) | copy-start | bytes 28
  7.2 98.9 %copy-start.4 = (bf16[1,128,2048]{2,1,0:T(8,128)(2,1)S(1)}, bf16[1,128,2048]{2,1,0:T(8,128)(2,1)}, u32[]{:S(2)}) copy-start(bf16[1,128,2048]{2,1,0:T(8,128)(2,1)} %param.9) | copy-start | bytes 1572868
  7.2 92.9 %all-gather.18.cloned.1.call-start = ((), (), s32[]{:S(2)}) async-start(), calls=%async_computation.3 | async-start | bytes 2129920 | tf_op jit(solution)/shard_map/all_gather | solution.py:33
  8.7 175.1 %all-gather.12.cloned.1.call-start = ((), (), s32[]{:S(2)}) async-start(), calls=%async_computation | async-start | bytes 2129920 | tf_op jit(solution)/shard_map/all_gather | solution.py:41
  100.1 6.7 %copy-start.2 = (bf16[1,1,1024,1024]{3,2,1,0:T(8,128)(2,1)S(1)}, bf16[1,1,1024,1024]{3,2,1,0:T(8,128)(2,1)}, u32[]{:S(2)}) copy-start(bf16[1,1,1024,1024]{3,2,1,0:T(8,128)(2,1)} %all-gather.18.cloned.1.call-done) | copy-start | bytes 6291460
  102.5 83.7 %copy-start.5 = (bf16[24,1024]{1,0:T(8,128)(2,1)}, bf16[24,1024]{1,0:T(8,128)(2,1)S(1)}, u32[]{:S(2)}) copy-start(bf16[24,1024]{1,0:T(8,128)(2,1)S(1)} %fusion.27) | copy-start | bytes 147460
  103.2 164.8 %all-gather.20.cloned.1.call-start = ((), (), s32[]{:S(2)}) async-start(), calls=%async_computation.4 | async-start | bytes 2129920 | tf_op jit(solution)/shard_map/all_gather | solution.py:33
  103.9 247.6 %all-gather.22.cloned.1.call-start = ((), (), s32[]{:S(2)}) async-start(), calls=%async_computation.5 | async-start | bytes 2129920 | tf_op jit(solution)/shard_map/all_gather | solution.py:33
  105.4 330.1 %all-gather.14.cloned.1.call-start = ((), (), s32[]{:S(2)}) async-start(), calls=%async_computation.1 | async-start | bytes 2129920 | tf_op jit(solution)/shard_map/all_gather | solution.py:41
  183.8 2.4 copy-start.3
  187.1 83.2 %slice-start = ((bf16[24,1024]{1,0:T(8,128)(2,1)}), bf16[8,1024]{1,0:T(8,128)(2,1)S(1)}, s32[]{:S(2)}) async-start(bf16[24,1024]{1,0:T(8,128)(2,1)} %copy-done.5), calls=%async_computation.7 | async-start | bytes 32768 | tf_op jit(solution)/shard_map/slice | solution.py:70
  268.0 86.4 %copy-start.8 = (s32[1,128]{1,0:T(1,128)S(1)}, s32[1,128]{1,0:T(1,128)}, u32[]{:S(2)}) copy-start(s32[1,128]{1,0:T(1,128)} %param.14) | copy-start | bytes 1540
  270.3 84.2 %copy-start.1 = (bf16[1,1,1024,1024]{3,2,1,0:T(8,128)(2,1)S(1)}, bf16[1,1,1024,1024]{3,2,1,0:T(8,128)(2,1)}, u32[]{:S(2)}) copy-start(bf16[1,1,1024,1024]{3,2,1,0:T(8,128)(2,1)} %all-gather.20.cloned.1.call-done) | copy-start | bytes 6291460
  270.9 248.0 %all-gather.24.cloned.1.call-start = ((), (), s32[]{:S(2)}) async-start(), calls=%async_computation.6 | async-start | bytes 2129920 | tf_op jit(solution)/shard_map/all_gather | solution.py:33
  271.5 331.1 %all-gather.16.cloned.1.call-start = ((), (), s32[]{:S(2)}) async-start(), calls=%async_computation.2 | async-start | bytes 2129920 | tf_op jit(solution)/shard_map/all_gather | solution.py:41
  355.3 87.6 %copy-start.6 = (bf16[1,128,2048]{2,1,0:T(8,128)(2,1)S(1)}, bf16[1,128,2048]{2,1,0:T(8,128)(2,1)}, u32[]{:S(2)}) copy-start(bf16[1,128,2048]{2,1,0:T(8,128)(2,1)} %param.15) | copy-start | bytes 1572868
  439.4 3.4 collective-permute-start
Sparse Core Ops, SparseCore 0:
  11.7 88.3 all-gather.17
  103.3 80.4 all-gather.11
  187.5 80.4 all-gather.19
  270.9 80.4 all-gather.21
  354.9 80.4 all-gather.13
  438.4 80.4 all-gather.23
  522.0 80.4 all-gather.15
where the time goes:
time: 614 us
  waiting for transfers between devices  566 us (92%)
  matrix products  21.5 us (4%)
  between operations  14.4 us (2%)
    all_gather x4, waiting for transfers between devices, apply_inverse(): lax.all_gather(inverse_shard, 'col', axis=0, tiled=True)  325 us
    all_gather x3, waiting for transfers between devices, apply_factor(): lax.all_gather(factor_shard, 'col', axis=0, tiled=True)  239 us
    dot_general x10, matrix products, times_rows(): lax.dot_general(left_rows, segment, (((1,), (1,)), ((), ())), preferred_e...  21.5 us
  transfers between devices with their start and end apart: 8, of which 8 were waited for; matrix products, arithmetic and copies ran while one was open for 4% of the time, Pallas kernels for 0%

commit v1 on v0

--- a/solution.py
+++ b/solution.py
@@ -30,7 +30,12 @@
     def apply_segment(segment, offset):
         return all_products(body_rows, extra_rows, segment)
 
-    return apply_segment(lax.all_gather(inverse_shard, "col", axis=0, tiled=True), jnp.int32(0))
+    return apply_segment(
+        jnp.concatenate(
+            lax.all_to_all(jnp.stack([inverse_shard] * lax.axis_size("col")), "col", 0, 0), axis=0
+        ),
+        jnp.int32(0),
+    )
 
 
 def apply_factor(body_rows, extra_rows, factor_shard):

time: 614 us -> 442 us (0.72)
  waiting for transfers between devices: 566 us -> 347 us
  starting transfers between devices: 2.2 us -> 45.9 us
    all_gather x4 -> x0, waiting for transfers between devices: 325 us -> none  [apply_inverse(): lax.all_gather(inverse_shard, 'col', axis=0, tiled=True)]
    all_to_all x0 -> x4, waiting for transfers between devices: none -> 99 us  [apply_inverse(): lax.all_to_all(jnp.stack([inverse_shard] * lax.axis_size('col')), 'col',...]
    all_to_all x0 -> x4, starting transfers between devices: none -> 43.9 us  [apply_inverse(): lax.all_to_all(jnp.stack([inverse_shard] * lax.axis_size('col')), 'col',...]
    all_gather x3, waiting for transfers between devices: 239 us -> 248 us  [apply_factor(): lax.all_gather(factor_shard, 'col', axis=0, tiled=True)]
    another operation x0 -> x5, local copies, waits for them, and re-layouts: none -> 7.24 us  [apply_inverse(): jnp.stack([inverse_shard] * lax.axis_size('col'))]
  transfers between devices with their start and end apart: 8 -> 8, of which waited for: 8 -> 6; matrix products, arithmetic and copies ran while one was open for 4% -> 5% of each run, Pallas kernels for 0% -> 0%
where the time goes in v1:
time: 442 us; the launch traced here: 441 us
  waiting for transfers between devices  347 us (79%)
  starting transfers between devices  45.9 us (10%)
  matrix products  19.8 us (4%)
  between operations  14 us (3%)
  local copies, waits for them, and re-layouts  9.45 us (2%)
  other arithmetic  4.45 us (1%)
    all_gather x3, waiting for transfers between devices, apply_factor(): lax.all_gather(factor_shard, 'col', axis=0, tiled=True)  248 us
    all_to_all x4, waiting for transfers between devices, apply_inverse(): lax.all_to_all(jnp.stack([inverse_shard] * lax.axis_size('col')), 'col',...  99 us
    all_to_all x4, starting transfers between devices, apply_inverse(): lax.all_to_all(jnp.stack([inverse_shard] * lax.axis_size('col')), 'col',...  43.9 us
    dot_general x10, matrix products, times_rows(): lax.dot_general(left_rows, segment, (((1,), (1,)), ((), ())), preferred_e...  19.8 us
  transfers between devices with their start and end apart: 8, of which 6 were waited for; matrix products, arithmetic and copies ran while one was open for 5% of the time, Pallas kernels for 0%

profile of v1, /device:TPU:2, one launch (start us, length us, event | category | flops | bytes accessed | tf_op | source)
XLA Modules:
  0.0 441.0 jit_solution(9077651866294370371)
XLA Ops:
  7.2 0.8 slice_bitcast_fusion.1
  8.0 1.6 stack.12
  9.6 16.7 %all-to-all-start = ((bf16[64,16,1024]{2,1,0:T(8,128)(2,1)}), bf16[64,16,1024]{2,1,0:T(8,128)(2,1)S(1)}, u32[]{:S(2)}, u32[]{:S(2)}) async-start(bf16[64,16,1024]{2,1,0:T(8,128)(2,1)} %stack.12), calls=%async_computation | async-start | bytes 4194304 | tf_op jit(solution)/shard_map/all_to_all | solution.py:35
  26.4 52.3 %all-to-all-done = bf16[64,16,1024]{2,1,0:T(8,128)(2,1)S(1)} async-done(((bf16[64,16,1024]{2,1,0:T(8,128)(2,1)}), bf16[64,16,1024]{2,1,0:T(8,128)(2,1)S(1)}, u32[]{:S(2)}, u32[]{:S(2)}) %all-to-all-start) | async-done | bytes 2097184 | tf_op jit(solution)/shard_map/all_to_all | solution.py:35
  78.7 0.7 convolution_convert_fusion.4
  79.4 0.7 slice.98
  80.1 1.6 stack.13
  81.7 9.2 %all-to-all-start.1 = ((bf16[64,16,1024]{2,1,0:T(8,128)(2,1)}), bf16[64,16,1024]{2,1,0:T(8,128)(2,1)S(1)}, u32[]{:S(2)}, u32[]{:S(2)}) async-start(bf16[64,16,1024]{2,1,0:T(8,128)(2,1)} %stack.13), calls=%async_computation.1 | async-start | bytes 4194304 | tf_op jit(solution)/shard_map/all_to_all | solution.py:35
  90.9 0.6 fusion.37
  91.6 0.8 dynamic-slice_bitcast_fusion.2
  93.0 3.0 convolution_convert_fusion.3
  96.0 99.4 %all-gather.4.cloned.1.call-done = bf16[1024,1024]{1,0:T(8,128)(2,1)} async-done(((bf16[16,1024]{1,0:T(8,128)(2,1)}), bf16[1024,1024]{1,0:T(8,128)(2,1)}) %all-gather.4.cloned.1.call-update) | async-done | bytes 2097168 | tf_op jit(solution)/shard_map/all_gather | solution.py:46
  195.4 2.4 fusion.34
  197.8 0.9 fusion.38
  198.7 1.6 stack.14
  200.3 9.0 %all-to-all-start.2 = ((bf16[64,16,1024]{2,1,0:T(8,128)(2,1)}), bf16[64,16,1024]{2,1,0:T(8,128)(2,1)}, u32[]{:S(2)}, u32[]{:S(2)}) async-start(bf16[64,16,1024]{2,1,0:T(8,128)(2,1)} %stack.14), calls=%async_computation.2 | async-start | bytes 4194304 | tf_op jit(solution)/shard_map/all_to_all | solution.py:35
  209.4 0.6 convolution_convert_fusion.6
  210.7 46.7 %all-to-all-done.2 = bf16[64,16,1024]{2,1,0:T(8,128)(2,1)} async-done(((bf16[64,16,1024]{2,1,0:T(8,128)(2,1)}), bf16[64,16,1024]{2,1,0:T(8,128)(2,1)}, u32[]{:S(2)}, u32[]{:S(2)}) %all-to-all-start.2) | async-done | bytes 2097184 | tf_op jit(solution)/shard_map/all_to_all | solution.py:35
  257.4 1.6 stack.15
  259.0 8.9 %all-to-all-start.3 = ((bf16[64,16,1024]{2,1,0:T(8,128)(2,1)}), bf16[64,16,1024]{2,1,0:T(8,128)(2,1)}, u32[]{:S(2)}, u32[]{:S(2)}) async-start(bf16[64,16,1024]{2,1,0:T(8,128)(2,1)} %stack.15), calls=%async_computation.3 | async-start | bytes 4194304 | tf_op jit(solution)/shard_map/all_to_all | solution.py:35
  268.0 2.9 convolution_convert_fusion.5
  271.0 0.8 convolution_convert_fusion.2
  271.8 74.4 %all-gather.6.cloned.1.call-done = bf16[512,2048]{1,0:T(8,128)(2,1)} async-done(((bf16[8,2048]{1,0:T(8,128)(2,1)}), bf16[512,2048]{1,0:T(8,128)(2,1)}) %all-gather.6.cloned.1.call-update) | async-done | bytes 2097168 | tf_op jit(solution)/shard_map/all_gather | solution.py:46
  346.3 2.4 convolution_negate_fusion
  348.7 1.5 scatter_custom_fusion
  350.2 1.9 collective-permute-start
  352.1 0.8 fusion.5
  353.0 0.7 collective-permute-done
  353.6 2.4 convolution_convert_fusion.1
  356.1 73.8 %all-gather.8.cloned.1.call-done = bf16[1024,1024]{1,0:T(8,128)(2,1)} async-done(((bf16[16,1024]{1,0:T(8,128)(2,1)}), bf16[1024,1024]{1,0:T(8,128)(2,1)}) %all-gather.8.cloned.1.call-update) | async-done | bytes 2097168 | tf_op jit(solution)/shard_map/all_gather | solution.py:46
  429.9 3.7 convolution_convert_fusion
  433.6 0.8 maximum_bitcast_fusion
  (37 shorter events, 1.6 us)
Async XLA Ops:
  7.2 260.8 %copy-start = (bf16[4,16,1024]{2,1,0:T(8,128)(2,1)S(1)}, bf16[4,16,1024]{2,1,0:T(8,128)(2,1)}, u32[]{:S(2)}) copy-start(bf16[4,16,1024]{2,1,0:T(8,128)(2,1)} %param.16) | copy-start | bytes 393220
  9.6 16.8 %copy-start.7 = (bf16[1,8,2048]{2,1,0:T(8,128)(2,1)S(1)}, bf16[1,8,2048]{2,1,0:T(8,128)(2,1)}, u32[]{:S(2)}) copy-start(bf16[1,8,2048]{2,1,0:T(8,128)(2,1)} %param.10) | copy-start | bytes 98308
  9.6 69.1 %copy-start.6 = (bf16[1,16,1024]{2,1,0:T(8,128)(2,1)S(1)}, bf16[1,16,1024]{2,1,0:T(8,128)(2,1)}, u32[]{:S(2)}) copy-start(bf16[1,16,1024]{2,1,0:T(8,128)(2,1)} %param.11) | copy-start | bytes 98308
  9.6 69.1 %all-to-all-start = ((bf16[64,16,1024]{2,1,0:T(8,128)(2,1)}), bf16[64,16,1024]{2,1,0:T(8,128)(2,1)S(1)}, u32[]{:S(2)}, u32[]{:S(2)}) async-start(bf16[64,16,1024]{2,1,0:T(8,128)(2,1)} %stack.12), calls=%async_computation | async-start | bytes 4194304 | tf_op jit(solution)/shard_map/all_to_all | solution.py:35
  26.3 169.1 %all-gather.4.cloned.1.call-start = ((), (), s32[]{:S(2)}) async-start(), calls=%async_computation.4 | async-start | bytes 2129920 | tf_op jit(solution)/shard_map/all_gather | solution.py:46
  78.7 2.9 copy-start.1
  79.4 116.0 %copy-start.4 = (bf16[24,1024]{1,0:T(8,128)(2,1)}, bf16[24,1024]{1,0:T(8,128)(2,1)S(1)}, u32[]{:S(2)}) copy-start(bf16[24,1024]{1,0:T(8,128)(2,1)S(1)} %convolution_convert_fusion.4) | copy-start | bytes 147460
  81.7 9.3 %copy-start.8 = (s32[1,1,2]{2,1,0:T(1,128)S(1)}, s32[1,1,2]{2,1,0:T(1,128)}, u32[]{:S(2)}) copy-start(s32[1,1,2]{2,1,0:T(1,128)} %param.13) | copy-start | bytes 28
  81.7 10.7 %copy-start.3 = (bf16[1,128,2048]{2,1,0:T(8,128)(2,1)S(1)}, bf16[1,128,2048]{2,1,0:T(8,128)(2,1)}, u32[]{:S(2)}) copy-start(bf16[1,128,2048]{2,1,0:T(8,128)(2,1)} %param.9) | copy-start | bytes 1572868
  81.7 117.0 %all-to-all-start.1 = ((bf16[64,16,1024]{2,1,0:T(8,128)(2,1)}), bf16[64,16,1024]{2,1,0:T(8,128)(2,1)S(1)}, u32[]{:S(2)}, u32[]{:S(2)}) async-start(bf16[64,16,1024]{2,1,0:T(8,128)(2,1)} %stack.13), calls=%async_computation.1 | async-start | bytes 4194304 | tf_op jit(solution)/shard_map/all_to_all | solution.py:35
  195.4 2.4 copy-start.2
  200.3 57.1 %all-to-all-start.2 = ((bf16[64,16,1024]{2,1,0:T(8,128)(2,1)}), bf16[64,16,1024]{2,1,0:T(8,128)(2,1)}, u32[]{:S(2)}, u32[]{:S(2)}) async-start(bf16[64,16,1024]{2,1,0:T(8,128)(2,1)} %stack.14), calls=%async_computation.2 | async-start | bytes 4194304 | tf_op jit(solution)/shard_map/all_to_all | solution.py:35
  209.3 0.7 slice-start
  209.3 137.0 %all-gather.6.cloned.1.call-start = ((), (), s32[]{:S(2)}) async-start(), calls=%async_computation.5 | async-start | bytes 2129920 | tf_op jit(solution)/shard_map/all_gather | solution.py:46
  259.0 97.1 %all-to-all-start.3 = ((bf16[64,16,1024]{2,1,0:T(8,128)(2,1)}), bf16[64,16,1024]{2,1,0:T(8,128)(2,1)}, u32[]{:S(2)}, u32[]{:S(2)}) async-start(bf16[64,16,1024]{2,1,0:T(8,128)(2,1)} %stack.15), calls=%async_computation.3 | async-start | bytes 4194304 | tf_op jit(solution)/shard_map/all_to_all | solution.py:35
  267.9 3.0 copy-start.9
  267.9 161.9 %all-gather.8.cloned.1.call-start = ((), (), s32[]{:S(2)}) async-start(), calls=%async_computation.6 | async-start | bytes 2129920 | tf_op jit(solution)/shard_map/all_gather | solution.py:46
  271.8 81.8 %copy-start.5 = (bf16[1,128,2048]{2,1,0:T(8,128)(2,1)S(1)}, bf16[1,128,2048]{2,1,0:T(8,128)(2,1)}, u32[]{:S(2)}) copy-start(bf16[1,128,2048]{2,1,0:T(8,128)(2,1)} %param.15) | copy-start | bytes 1572868
  350.2 3.4 collective-permute-start
Sparse Core Ops, SparseCore 0:
  80.2 115.1 all-gather.3
  213.8 132.4 all-gather.5
  349.3 80.4 all-gather.7
